TPU v7x, 32 devices: a whole 2x2x4 slice. The times are simulated.
32 devices in a mesh: ctx: 8 (over z, x), ch: 4 (over y, core).
Axes of the slice: x: 2, y: 2, z: 4, core: 2. Of those that a mesh axis runs over, the one named last changes fastest.
Arguments:
- tokens: bfloat16 [4096, 8192], P('ctx'), may hold values from -6 to 6
- in_weight: bfloat16 [8192, 3, 4096], P('ctx', None, 'ch'), may hold values from -0.0625 to 0.0625
- short_taps: float32 [3, 3, 4096], P(None, None, 'ch'), may hold values from -3 to 3
- decay_rates: float32 [16, 4096], P(None, 'ch'), may hold values from 0 to 0.034, as said below
- residues: float32 [16, 4096], P(None, 'ch'), may hold values from -1.5 to 1.5
Outputs:
- mixed: bfloat16 [4096, 4096], P(('ctx', 'ch'))
Inputs may be any that keep to these rules, and one draw needn't show every extreme that they name: `decay_rates`: positive decay rates.
All inputs are finite; a program needn't handle non-finite values.
Results may differ from a plain program's by a relative error of at most 0.0063.
Values may be sent and summed in bfloat16 or wider, within the bound.
No kernel may reach another device: no remote copies, remote signals or barrier semaphores. Data moves between devices by JAX's collectives and lax.ppermute only.
A program may use at most 128 MiB of HBM per device.

v0:
```python
import jax
import jax.numpy as jnp
from jax import lax
from jax.sharding import PartitionSpec as P


def shifted(value, axis, steps):
    count = lax.axis_size(axis)
    initial, last = (max(0, -steps), min(count, count - steps))
    return lax.ppermute(value, axis, [(source, source + steps) for source in range(initial, last)])


def block_run(block_input, decay_rates, scaled, start_state, lower_tri):
    sub_len = block_input.shape[0]
    offsets = jnp.arange(1, sub_len + 1, dtype=jnp.float32)
    growth = jnp.exp(decay_rates[None] * offsets[:, None, None])
    shrink = jnp.exp(-decay_rates[None] * offsets[:, None, None])
    weighted = (block_input[:, None, :] * growth).reshape(sub_len, -1)
    summed = jnp.dot(lower_tri, weighted, precision=lax.Precision.HIGHEST).reshape(growth.shape)
    states = shrink * (start_state[None] + summed)
    conv_out = jnp.sum(scaled[None] * states, axis=1)
    return (conv_out, states[-1])


def run_blocks(all_input, decay_rates, scaled, start_state):
    row_count = all_input.shape[0]
    block_len = min(128, row_count)
    lower_tri = (jnp.arange(block_len)[:, None] >= jnp.arange(block_len)[None, :]).astype(
        jnp.float32
    )

    def run_sub_step(carried, block_input):
        conv_out, last_state = block_run(block_input, decay_rates, scaled, carried, lower_tri)
        return (last_state, conv_out)

    last_state, conv_out = lax.scan(
        run_sub_step, start_state, all_input.reshape(row_count // block_len, block_len, -1)
    )
    return (conv_out.reshape(row_count, -1), last_state)


def block_end(all_input, decay_rates):
    row_count = all_input.shape[0]
    block_len = min(128, row_count)
    lag_table = jnp.arange(block_len - 1, -1, -1, dtype=jnp.float32)
    lag_weights = jnp.exp(-decay_rates[None] * lag_table[:, None, None])
    jump_decay = jnp.exp(-decay_rates * block_len)

    def block_sub_step(carried, block_input):
        return (jump_decay * carried + jnp.sum(lag_weights * block_input[:, None, :], axis=0), None)

    last_state, unused = lax.scan(
        block_sub_step,
        jnp.zeros_like(decay_rates),
        all_input.reshape(row_count // block_len, block_len, -1),
    )
    return last_state


def shards(tokens, in_weight, short_taps, decay_rates, residues):
    tok_rows = tokens.shape[0]
    chan_count = in_weight.shape[2]
    gathered = lax.all_gather(in_weight, "ctx", axis=0, tiled=True)
    projected = jnp.dot(
        tokens, gathered.reshape(gathered.shape[0], -1), preferred_element_type=jnp.float32
    )
    projected = projected.astype(jnp.bfloat16).reshape(tok_rows, 3, chan_count)
    before = shifted(projected[tok_rows - 2 :], "ctx", 1)
    extended = jnp.concatenate([before, projected], axis=0).astype(jnp.float32)
    featurized = (
        short_taps[0] * extended[2:]
        + short_taps[1] * extended[1:-1]
        + short_taps[2] * extended[:-2]
    )
    query_part = featurized[:, 0]
    product = featurized[:, 1] * featurized[:, 2]
    scaled = residues * jnp.sqrt(2.0 * decay_rates)
    decay_block = jnp.exp(-decay_rates * tok_rows)
    local_end = block_end(product, decay_rates)

    def chain_step(step_index, incoming):
        return shifted(decay_block * incoming + local_end, "ctx", 1)

    incoming = lax.fori_loop(0, lax.axis_size("ctx") - 1, chain_step, jnp.zeros_like(decay_rates))
    conv_out, last_state = run_blocks(product, decay_rates, scaled, incoming)
    gated_out = (query_part * conv_out).astype(jnp.bfloat16)
    return lax.all_to_all(gated_out, "ch", split_axis=0, concat_axis=1, tiled=True)


def solution(mesh):
    return jax.shard_map(
        shards,
        mesh=mesh,
        in_specs=(
            P("ctx", None),
            P("ctx", None, "ch"),
            P(None, None, "ch"),
            P(None, "ch"),
            P(None, "ch"),
        ),
        out_specs=P(("ctx", "ch"), None),
        check_vma=False,
    )
```

profile of v0, /device:TPU:0, one launch (start us, length us, event | category | flops | bytes accessed | tf_op | source)
XLA Modules:
  0.0 1266.5 jit_solution(5056268939107699735)
XLA Ops:
  6.5 8.7 copy.17
  16.5 953.9 %all-gather.2.cloned.1.call-done = bf16[8192,3,1024]{0,2,1:T(8,128)(2,1)} async-done(((bf16[1024,3,1024]{0,2,1:T(8,128)(2,1)}), bf16[8192,3,1024]{0,2,1:T(8,128)(2,1)}) %all-gather.2.cloned.1.call-update) | async-done | bytes 50331664 | tf_op jit(solution)/shard_map/all_gather | solution.py:63
  970.4 33.0 %convolution_convert_fusion = bf16[512,3072]{1,0:T(8,128)(2,1)S(1)} fusion(bf16[512,8192]{1,0:T(8,128)(2,1)} %param.11, bf16[8192,3072]{0,1:T(8,128)(2,1)} %bitcast.63), kind=kOutput, calls=%fused_computation.27 | convolution fusion | flops 25771376640 | bytes 61865984 | tf_op jit(solution)/shard_map/dot_general | solution.py:64
  1017.1 5.6 fusion.13
  1027.4 7.0 while.37
  1034.4 46.4 %while.35 = (s32[]{:T(128)}, f32[16,1024]{1,0:T(8,128)S(1)}, f32[16,1024]{1,0:T(8,128)S(1)}, f32[16,1024]{1,0:T(8,128)S(1)}, s32[]{:T(128)}) while((s32[]{:T(128)}, f32[16,1024]{1,0:T(8,128)S(1)}, f32[16,1024]{1,0:T(8,128)S(1)}, f32[16,1024]{1,0:T(8,128)S(1)}, s32[]{:T(128)}) %tuple.72), condition=%wide.region_4.5_spmd, body=%wide.region_3.4_spmd.sunk | while | flops 32770 | bytes 524389 | solution.py:84
  1080.8 157.0 %while.36 = (s32[]{:T(128)}, f32[16,1024]{1,0:T(8,128)S(1)}, f32[4,128,1024]{2,1,0:T(8,128)}, f32[1,16,1024]{2,1,0:T(8,128)S(1)}, f32[4,128,1024]{2,1,0:T(8,128)...) while((s32[]{:T(128)}, f32[16,1024]{1,0:T(8,128)S(1)}, ...), condition=%wide.region_7.8_spmd.clone, body=%wide.region_5.7_spmd.clone.sunk | while | flops 3235807488 | bytes 79169624 | solution.py:36
  1081.9 7.1 copy.32
  1089.1 15.7 %fusion.24 = f32[16384,128]{1,0:T(8,128)} fusion(f32[128,16384]{1,0:T(8,128)S(1)} %bitcast.53, f32[128]{0:T(128)S(1)} %iota_add_fusion.2, f32[16384]{0:T(1024)S(1)} %bitcast.58), kind=kOutput, calls=%fused_computation.5.clone.1 | convolution fusion | flops 3225452544 | bytes 16843264 | tf_op jit(solution)/shard_map/while/body/eval_jaxpr/dot_general | solution.py:19
  1104.8 8.8 copy.34
  1113.6 5.6 multiply_reduce_fusion.2
  1121.2 7.1 copy.32
  1128.3 15.7 %fusion.24 = f32[16384,128]{1,0:T(8,128)} fusion(f32[128,16384]{1,0:T(8,128)S(1)} %bitcast.53, f32[128]{0:T(128)S(1)} %iota_add_fusion.2, f32[16384]{0:T(1024)S(1)} %bitcast.58), kind=kOutput, calls=%fused_computation.5.clone.1 | convolution fusion | flops 3225452544 | bytes 16843264 | tf_op jit(solution)/shard_map/while/body/eval_jaxpr/dot_general | solution.py:19
  1144.1 8.8 copy.34
  1152.9 5.6 multiply_reduce_fusion.2
  1160.4 7.1 copy.32
  1167.6 15.7 %fusion.24 = f32[16384,128]{1,0:T(8,128)} fusion(f32[128,16384]{1,0:T(8,128)S(1)} %bitcast.53, f32[128]{0:T(128)S(1)} %iota_add_fusion.2, f32[16384]{0:T(1024)S(1)} %bitcast.58), kind=kOutput, calls=%fused_computation.5.clone.1 | convolution fusion | flops 3225452544 | bytes 16843264 | tf_op jit(solution)/shard_map/while/body/eval_jaxpr/dot_general | solution.py:19
  1183.3 8.8 copy.34
  1192.1 5.6 multiply_reduce_fusion.2
  1199.6 7.1 copy.32
  1206.8 15.7 %fusion.24 = f32[16384,128]{1,0:T(8,128)} fusion(f32[128,16384]{1,0:T(8,128)S(1)} %bitcast.53, f32[128]{0:T(128)S(1)} %iota_add_fusion.2, f32[16384]{0:T(1024)S(1)} %bitcast.58), kind=kOutput, calls=%fused_computation.5.clone.1 | convolution fusion | flops 3225452544 | bytes 16843264 | tf_op jit(solution)/shard_map/while/body/eval_jaxpr/dot_general | solution.py:19
  1222.6 8.8 copy.34
  1231.4 5.6 multiply_reduce_fusion.2
  1241.6 17.0 %all_to_all.16 = bf16[4,128,1024]{2,1,0:T(8,128)(2,1)S(1)} all-to-all(bf16[4,128,1024]{2,1,0:T(8,128)(2,1)S(1)} %multiply_convert_fusion), channel_id=1, replica_groups=mesh['ctx'=8,'ch'=4] {'ch'}, dimensions={0} | all-to-all | bytes 2097152 | tf_op jit(solution)/shard_map/all_to_all | solution.py:87
  (93 shorter events, 85.5 us)
Async XLA Ops:
  6.5 8.7 copy-start.6
  6.5 9.3 copy-start.1
  6.5 9.3 copy-start.2
  6.5 963.9 %all-gather.2.cloned.1.call-start = ((), (), s32[]{:S(2)}) async-start(), calls=%async_computation.1 | async-start | bytes 56623104 | tf_op jit(solution)/shard_map/all_gather | solution.py:63
  1003.4 1.6 copy-start
  1005.6 6.6 collective-permute-start.1
  1014.2 2.8 copy-start.4
  1014.2 2.9 copy-start.5
  1022.7 4.7 copy-start.3
  1022.7 4.7 copy-start.7
  1034.5 5.8 collective-permute-start
  1040.3 6.2 collective-permute-start
  1046.4 6.2 collective-permute-start
  1052.6 6.7 collective-permute-start
  1059.3 7.4 collective-permute-start
  1066.7 7.0 collective-permute-start
  1073.7 7.1 collective-permute-start
Sparse Core Ops, SparseCore 0:
  15.3 955.0 all-gather.1
where the time goes:
time: 1270 us
  waiting for transfers between devices  967 us (76%)
  matrix products  95.9 us (8%)
  local copies, waits for them, and re-layouts  93.3 us (7%)
  other arithmetic  43.4 us (3%)
  starting transfers between devices  35.6 us (3%)
  blocking collectives  17 us (1%)
  between operations  13.5 us (1%)
    all_gather x1, waiting for transfers between devices, shards(): gathered = lax.all_gather(in_weight, 'ctx', axis=0, tiled=True)  954 us
    dot_general x4, matrix products, block_run(): jnp.dot(lower_tri, weighted, precision=lax.Precision.HIGHEST)  62.9 us
    ppermute x8, starting transfers between devices, shifted(): lax.ppermute(value, axis, [(source, source + steps) for source in range(i...  35.6 us
    reshape x4, local copies, waits for them, and re-layouts, block_run(): jnp.dot(lower_tri, weighted, precision=lax.Precision.HIGHEST)  35.2 us
    dot_general x1, matrix products, shards(): jnp.dot(tokens, gathered.reshape(gathered.shape[0], -1), preferred_elemen...  33 us
    while x8, local copies, waits for them, and re-layouts  28.6 us
  transfers between devices with their start and end apart: 9, of which 8 were waited for; matrix products, arithmetic and copies ran while one was open for 0% of the time, Pallas kernels for 0%

commit v1 on v0

v1 whole, which is shorter than its diff:
```python
import functools

import jax
import jax.numpy as jnp
from jax import lax
from jax.experimental import pallas as pl
from jax.experimental.pallas import tpu as pltpu
from jax.sharding import Mesh
from jax.sharding import PartitionSpec as P


def conv_kernel(order, proj, taps, decay, scaled, state_in, halo_in, out, state, halo, ext, prod, modes):
    rows, width = out.shape[1], out.shape[2]
    mode_count = decay.shape[0]

    @pl.when(pl.program_id(0) == 0)
    def _():
        state[...] = state_in[...]
        halo[...] = halo_in[...]

    ext[0:8, :] = halo[...]
    ext[8 : 8 + rows, :] = proj[0].astype(jnp.float32)
    halo[...] = ext[rows : rows + 8, :]

    def branch(i):
        cols = slice(i * width, (i + 1) * width)
        return (
            taps[0:1, cols] * ext[8 : 8 + rows, cols]
            + taps[1:2, cols] * ext[7 : 7 + rows, cols]
            + taps[2:3, cols] * ext[6 : 6 + rows, cols]
        )

    prod[...] = branch(1) * branch(2)
    halves = [slice(s, s + 8) for s in range(0, mode_count, 8)]
    decays = [decay[h, :] for h in halves]
    scales = [scaled[h, :] for h in halves]

    def step(t, states):
        entry = jnp.broadcast_to(prod[pl.ds(t, 1), :], (8, width))
        states = tuple(d * s + entry for d, s in zip(decays, states))
        total = scales[0] * states[0]
        for c, s in zip(scales[1:], states[1:]):
            total = total + c * s
        modes[pl.ds(pl.multiple_of(t * 8, 8), 8), :] = total
        return states

    states = lax.fori_loop(0, rows, step, tuple(state[h, :] for h in halves), unroll=8)
    for h, s in zip(halves, states):
        state[h, :] = s
    conv = modes[pl.ds(0, rows, stride=8), :]
    for s in range(1, 8):
        conv = conv + modes[pl.ds(s, rows, stride=8), :]
    out[0] = (branch(0) * conv).astype(out.dtype)


def run_conv(order, proj, taps, decay, scaled, state, halo):
    blocks, rows, width3 = proj.shape
    width = width3 // 3
    mode_count = decay.shape[0]
    whole = lambda shape: pl.BlockSpec(shape, lambda i, order: (0,) * len(shape))
    return pl.pallas_call(
        conv_kernel,
        out_shape=(
            jax.ShapeDtypeStruct((blocks, rows, width), jnp.bfloat16),
            jax.ShapeDtypeStruct((mode_count, width), jnp.float32),
            jax.ShapeDtypeStruct((8, width3), jnp.float32),
        ),
        grid_spec=pltpu.PrefetchScalarGridSpec(
            num_scalar_prefetch=1,
            grid=(blocks,),
            in_specs=[
                pl.BlockSpec((1, rows, width3), lambda i, order: (order[i], 0, 0)),
                whole((3, width3)),
                whole((mode_count, width)),
                whole((mode_count, width)),
                whole((mode_count, width)),
                whole((8, width3)),
            ],
            out_specs=[
                pl.BlockSpec((1, rows, width), lambda i, order: (i, 0, 0)),
                whole((mode_count, width)),
                whole((8, width3)),
            ],
            scratch_shapes=[
                pltpu.VMEM((rows + 8, width3), jnp.float32),
                pltpu.VMEM((rows, width), jnp.float32),
                pltpu.VMEM((rows * 8, width), jnp.float32),
            ],
        ),
        compiler_params=pltpu.CompilerParams(vmem_limit_bytes=24 * 1024 * 1024),
        cost_estimate=pl.CostEstimate(
            flops=8 * blocks * rows * mode_count * width,
            bytes_accessed=blocks * rows * width * 8,
            transcendentals=0,
        ),
    )(order, proj, taps, decay, scaled, state, halo)


def gather_rel(value, axis):
    count = lax.axis_size(axis)
    pieces = [value]
    for k in range(1, count):
        pieces.append(lax.ppermute(value, axis, [(s, (s + k) % count) for s in range(count)]))
    return jnp.concatenate(pieces, axis=0) if count > 1 else value


def shards(tokens, in_weight, short_taps, decay_rates, residues):
    Z, X, Y, C = (lax.axis_size(a) for a in ("z", "x", "y", "c"))
    z, x, y, c = (lax.axis_index(a) for a in ("z", "x", "y", "c"))
    tok_rows, depth = tokens.shape
    w_rows, _, chans = in_weight.shape
    own = chans // X
    half = own // 2
    groups = max(1, half // 128)
    width = half // groups
    plane_depth = X * w_rows

    lower = z < Z // 2
    far_off = jnp.where(lower, 0, half)
    near_off = half - far_off

    weight = jnp.transpose(in_weight, (1, 0, 2))

    def part(target, g):
        cuts = [
            lax.dynamic_slice(weight, (i, 0, target * own + off + g * width), (1, w_rows, width))[0]
            for off in (far_off, near_off)
            for i in range(3)
        ]
        return jnp.concatenate(cuts, axis=1)

    weights = []
    for g in range(groups):
        held = jnp.zeros((X, w_rows, 6 * width), in_weight.dtype)
        held = lax.dynamic_update_slice(held, part(x, g)[None], (x, 0, 0))
        for k in range(1, X):
            got = lax.ppermute(
                part((x + k) % X, g), "x", [(s, (s + k) % X) for s in range(X)]
            )
            held = lax.dynamic_update_slice(held, got[None], ((x + X - k) % X, 0, 0))
        weights.append(held.reshape(plane_depth, 6 * width))

    share = tok_rows // (Y * C)
    mine = lax.dynamic_slice(tokens, ((y * C + c) * share, 0), (share, depth))
    mine = mine.reshape(share, Z, plane_depth).transpose(1, 0, 2)
    split = lax.all_to_all(mine, "z", split_axis=0, concat_axis=0, tiled=True)

    bx, by, bc = jnp.meshgrid(jnp.arange(X), jnp.arange(Y), jnp.arange(C), indexing="ij")
    order = (((c - bc) % C) * Y + (y - by) % Y) * X + (x - bx) % X
    order = order.reshape(-1).astype(jnp.int32)

    def near_cut(value, g):
        return lax.dynamic_slice_in_dim(value, x * own + near_off + g * width, width, axis=value.ndim - 1)

    scaled_all = residues * jnp.sqrt(2.0 * decay_rates)
    decay_all = jnp.exp(-decay_rates)
    taps = [near_cut(short_taps, g).reshape(3, 3 * width) for g in range(groups)]
    decay = [near_cut(decay_all, g) for g in range(groups)]
    scaled = [near_cut(scaled_all, g) for g in range(groups)]
    state = [jnp.zeros_like(d) for d in decay]
    halo = [jnp.zeros((8, 3 * width), jnp.float32) for _ in range(groups)]

    outs = []
    for zt in range(Z):
        block = gather_rel(gather_rel(gather_rel(split[zt], "x"), "y"), "c")
        per_group = []
        for g in range(groups):
            partial = jnp.dot(block, weights[g], preferred_element_type=jnp.float32)
            far, near = partial[:, : 3 * width], partial[:, 3 * width :]
            got = None
            for hop in range(1, Z):
                send = far if hop <= Z // 2 else near
                if got is not None:
                    send = send + got.astype(jnp.float32)
                got = lax.ppermute(
                    send.astype(jnp.bfloat16), "z", [(hop - 1, hop), (Z - hop, Z - 1 - hop)]
                )
            total = (near + got.astype(jnp.float32)).astype(jnp.bfloat16)
            total = total.reshape(X * Y * C, share, 3 * width)
            out, state[g], halo[g] = run_conv(order, total, taps[g], decay[g], scaled[g], state[g], halo[g])
            per_group.append(out)
        outs.append(jnp.concatenate(per_group, axis=2))

    result = jnp.stack(outs).reshape(Z * X * Y * C, share, half)
    result = lax.all_to_all(result, ("z", "x", "y", "c"), split_axis=0, concat_axis=0, tiled=True)
    result = result.reshape(Z, X, Y, C, share, half)
    result = jnp.stack([result[Z - 1], result[0]])
    return result.transpose(4, 2, 3, 1, 0, 5).reshape(share, -1)


def solution(mesh):
    ctx, ch = mesh.shape["ctx"], mesh.shape["ch"]
    xs = 1
    while 4 * xs * xs <= ctx:
        xs *= 2
    cs = 2 if ch % 2 == 0 else 1
    fine = Mesh(mesh.devices.reshape(ctx // xs, xs, ch // cs, cs), ("z", "x", "y", "c"))
    return jax.shard_map(
        shards,
        mesh=fine,
        in_specs=(
            P(("z", "x"), None),
            P(("z", "x"), None, ("y", "c")),
            P(None, None, ("y", "c")),
            P(None, ("y", "c")),
            P(None, ("y", "c")),
        ),
        out_specs=P(("z", "x", "y", "c"), None),
        check_vma=False,
    )
```

time: 1270 us -> 601 us (0.47)
  waiting for transfers between devices: 967 us -> 343 us
  matrix products: 95.9 us -> 43.3 us
  local copies, waits for them, and re-layouts: 93.3 us -> 41.6 us
  Pallas kernels: 0 us -> 35.6 us
  blocking collectives: 17 us -> 52 us
  other arithmetic: 43.4 us -> 22.5 us
  starting transfers between devices: 35.6 us -> 52.3 us
    all_gather x1 -> x0, waiting for transfers between devices: 954 us -> none  [shards(): gathered = lax.all_gather(in_weight, 'ctx', axis=0, tiled=True)]
    ppermute x8 -> x38, waiting for transfers between devices: 13.4 us -> 309 us  [the longest x24 177 us: shards(): lax.ppermute(send.astype(jnp.bfloat16), 'z', [(hop - 1, hop), (Z - hop, Z...]
    dot_general x5 -> x8, matrix products: 95.9 us -> 43.3 us  [shards(): partial = jnp.dot(block, weights[g], preferred_element_type=jnp.float32)]
    pallas_call x0 -> x8, Pallas kernels: none -> 35.6 us  [run_conv(): pl.pallas_call(conv_kernel, out_shape=(jax.ShapeDtypeStruct((blocks, rows...]
    all_to_all x1, blocking collectives: 17 us -> 52 us  [shards(): lax.all_to_all(result, ('z', 'x', 'y', 'c'), split_axis=0, concat_axis=0,...]
    all_to_all x0 -> x1, waiting for transfers between devices: none -> 34.9 us  [shards(): split = lax.all_to_all(mine, 'z', split_axis=0, concat_axis=0, tiled=True)]
    reshape x4 -> x1, local copies, waits for them, and re-layouts: 35.2 us -> 1.61 us  [shards(): return result.transpose(4, 2, 3, 1, 0, 5).reshape(share, -1)]
    reduce_sum x8 -> x0, other arithmetic: 28.7 us -> none  [the longest x4 22.2 us: block_run(): conv_out = jnp.sum(scaled[None] * states, axis=1)]
  transfers between devices with their start and end apart: 9 -> 39, of which waited for: 8 -> 21; matrix products, arithmetic and copies ran while one was open for 0% -> 15% of each run, Pallas kernels for 0% -> 5%
where the time goes in v1:
time: 601 us; the launch traced here: 592 us
  waiting for transfers between devices  343 us (57%)
  starting transfers between devices  52.3 us (9%)
  blocking collectives  52 us (9%)
  matrix products  43.3 us (7%)
  local copies, waits for them, and re-layouts  41.6 us (7%)
  Pallas kernels  35.6 us (6%)
  other arithmetic  22.5 us (4%)
    ppermute x24, waiting for transfers between devices, shards(): lax.ppermute(send.astype(jnp.bfloat16), 'z', [(hop - 1, hop), (Z - hop, Z...  177 us
    ppermute x12, waiting for transfers between devices, gather_rel(): lax.ppermute(value, axis, [(s, (s + k) % count) for s in range(count)])  132 us
    all_to_all x1, blocking collectives, shards(): lax.all_to_all(result, ('z', 'x', 'y', 'c'), split_axis=0, concat_axis=0,...  52 us
    dot_general x8, matrix products, shards(): partial = jnp.dot(block, weights[g], preferred_element_type=jnp.float32)  43.3 us
    pallas_call x8, Pallas kernels, run_conv(): pl.pallas_call(conv_kernel, out_shape=(jax.ShapeDtypeStruct((blocks, rows...  35.6 us
    all_to_all x1, waiting for transfers between devices, shards(): split = lax.all_to_all(mine, 'z', split_axis=0, concat_axis=0, tiled=True)  34.9 us
    ppermute x24, starting transfers between devices, shards(): lax.ppermute(send.astype(jnp.bfloat16), 'z', [(hop - 1, hop), (Z - hop, Z...  33.5 us
    unnamed x34, local copies, waits for them, and re-layouts  20.1 us
  transfers between devices with their start and end apart: 39, of which 21 were waited for; matrix products, arithmetic and copies ran while one was open for 15% of the time, Pallas kernels for 5%

profile of v1, /device:TPU:0, one launch (start us, length us, event | category | flops | bytes accessed | tf_op | source)
XLA Modules:
  0.0 592.2 jit_solution(1269563734890641117)
XLA Ops:
  4.2 6.3 %all-to-all-start = ((bf16[4,128,2048]{1,2,0:T(8,128)(2,1)}), bf16[4,128,2048]{1,2,0:T(8,128)(2,1)S(1)}, u32[]{:S(2)}, u32[]{:S(2)}) async-start(bf16[4,128,2048]{1,2,0:T(8,128)(2,1)} %bitcast.120), calls=%async_computation | async-start | bytes 4194304 | tf_op jit(solution)/shard_map/all_to_all | solution.py:146
  23.9 34.9 %all-to-all-done = bf16[4,128,2048]{1,2,0:T(8,128)(2,1)S(1)} async-done(((bf16[4,128,2048]{1,2,0:T(8,128)(2,1)}), bf16[4,128,2048]{1,2,0:T(8,128)(2,1)S(1)}, u32[]{:S(2)}, u32[]{:S(2)}) %all-to-all-start) | async-done | bytes 2097184 | tf_op jit(solution)/shard_map/all_to_all | solution.py:146
  68.5 7.5 %collective-permute-done = bf16[128,2048]{1,0:T(8,128)(2,1)S(1)} collective-permute-done((bf16[128,2048]{1,0:T(8,128)(2,1)S(1)}, bf16[128,2048]{1,0:T(8,128)(2,1)S(1)}, u32[]{:S(2)}, u32[]{:S(2)}) %collective-permute-start) | collective-permute-done | bytes 524320 | tf_op jit(solution)/shard_map/ppermute | solution.py:103
  88.6 10.1 %collective-permute-done.1 = bf16[256,2048]{1,0:T(8,128)(2,1)} collective-permute-done((bf16[256,2048]{1,0:T(8,128)(2,1)}, bf16[256,2048]{1,0:T(8,128)(2,1)}, u32[]{:S(2)}, u32[]{:S(2)}) %collective-permute-start.1) | collective-permute-done | bytes 1048608 | tf_op jit(solution)/shard_map/ppermute | solution.py:103
  103.4 51.4 %collective-permute-done.11 = bf16[128,2048]{1,0:T(8,128)(2,1)} collective-permute-done((bf16[128,2048]{1,0:T(8,128)(2,1)S(1)}, bf16[128,2048]{1,0:T(8,128)(2,1)}, u32[]{:S(2)}, u32[]{:S(2)}) %collective-permute-start.11) | collective-permute-done | bytes 524320 | tf_op jit(solution)/shard_map/ppermute | solution.py:103
  157.1 8.8 %collective-permute-done.20 = bf16[128,2048]{1,0:T(8,128)(2,1)S(1)} collective-permute-done((bf16[128,2048]{1,0:T(8,128)(2,1)S(1)}, bf16[128,2048]{1,0:T(8,128)(2,1)S(1)}, u32[]{:S(2)}, u32[]{:S(2)}) %collective-permute-start.20) | collective-permute-done | bytes 524320 | tf_op jit(solution)/shard_map/ppermute | solution.py:103
  168.5 6.7 %collective-permute-done.29 = bf16[128,2048]{1,0:T(8,128)(2,1)S(1)} collective-permute-done((bf16[128,2048]{1,0:T(8,128)(2,1)S(1)}, bf16[128,2048]{1,0:T(8,128)(2,1)S(1)}, u32[]{:S(2)}, u32[]{:S(2)}) %collective-permute-start.29) | collective-permute-done | bytes 524320 | tf_op jit(solution)/shard_map/ppermute | solution.py:103
  181.9 10.4 %collective-permute-done.12 = bf16[256,2048]{1,0:T(8,128)(2,1)} collective-permute-done((bf16[256,2048]{1,0:T(8,128)(2,1)}, bf16[256,2048]{1,0:T(8,128)(2,1)}, u32[]{:S(2)}, u32[]{:S(2)}) %collective-permute-start.12) | collective-permute-done | bytes 1048608 | tf_op jit(solution)/shard_map/ppermute | solution.py:103
  194.0 20.8 %collective-permute-done.21 = bf16[256,2048]{1,0:T(8,128)(2,1)} collective-permute-done((bf16[256,2048]{1,0:T(8,128)(2,1)}, bf16[256,2048]{1,0:T(8,128)(2,1)}, u32[]{:S(2)}, u32[]{:S(2)}) %collective-permute-start.21) | collective-permute-done | bytes 1048608 | tf_op jit(solution)/shard_map/ppermute | solution.py:103
  216.4 15.9 %collective-permute-done.30 = bf16[256,2048]{1,0:T(8,128)(2,1)S(1)} collective-permute-done((bf16[256,2048]{1,0:T(8,128)(2,1)S(1)}, bf16[256,2048]{1,0:T(8,128)(2,1)S(1)}, u32[]{:S(2)}, u32[]{:S(2)}) %collective-permute-start.30) | collective-permute-done | bytes 1048608 | tf_op jit(solution)/shard_map/ppermute | solution.py:103
  233.3 6.4 %fusion.7 = f32[1024,768]{1,0:T(8,128)S(1)} fusion(bf16[2048,768]{1,0:T(8,128)(2,1)S(1)} %bitcast.146, bf16[512,2048]{1,0:T(8,128)(2,1)} %collective-permute-done.2, bf16[256,2048]{1,0:T(8,128)(2,1)} %collective-permute-done.1, bf16[128,2048]{1,0:T(8,128)(2,1)S(1)} %copy-done.6, bf16[128,2048]{1,0:T(8,128)(2,1)S(1)} %bitcast.125), kind=kOutput, calls=%fused_computation.57 | convolution fusion | flops 3238002688 | bytes 10485760 | tf_op jit(solution)/shard_map/dot_general | solution.py:168
  270.6 6.4 %fusion.2 = f32[1024,768]{1,0:T(8,128)S(1)} fusion(bf16[2048,768]{1,0:T(8,128)(2,1)S(1)} %bitcast.144, bf16[512,2048]{1,0:T(8,128)(2,1)} %copy-done.11, bf16[256,2048]{1,0:T(8,128)(2,1)} %collective-permute-done.21, bf16[128,2048]{1,0:T(8,128)(2,1)S(1)} %collective-permute-done.20, bf16[128,2048]{1,0:T(8,128)(2,1)S(1)} %bitcast.136), kind=kOutput, calls=%fused_computation.52 | convolution fusion | flops 3238002688 | bytes 10485760 | tf_op jit(solution)/shard_map/dot_general | solution.py:168
  299.7 11.0 %collective-permute-done.17 = bf16[1024,384]{1,0:T(8,128)(2,1)} collective-permute-done((bf16[1024,384]{1,0:T(8,128)(2,1)S(1)}, bf16[1024,384]{1,0:T(8,128)(2,1)}, u32[]{:S(2)}, u32[]{:S(2)}) %collective-permute-start.17) | collective-permute-done | bytes 786464 | tf_op jit(solution)/shard_map/ppermute | solution.py:175
  312.7 14.8 %collective-permute-done.23 = bf16[1024,384]{1,0:T(8,128)(2,1)S(1)} collective-permute-done((bf16[1024,384]{1,0:T(8,128)(2,1)S(1)}, bf16[1024,384]{1,0:T(8,128)(2,1)S(1)}, u32[]{:S(2)}, u32[]{:S(2)}) %collective-permute-start.23) | collective-permute-done | bytes 786464 | tf_op jit(solution)/shard_map/ppermute | solution.py:175
  328.5 15.9 %collective-permute-done.26 = bf16[1024,384]{1,0:T(8,128)(2,1)S(1)} collective-permute-done((bf16[1024,384]{1,0:T(8,128)(2,1)S(1)}, bf16[1024,384]{1,0:T(8,128)(2,1)S(1)}, u32[]{:S(2)}, u32[]{:S(2)}) %collective-permute-start.26) | collective-permute-done | bytes 786464 | tf_op jit(solution)/shard_map/ppermute | solution.py:175
  345.3 15.9 %collective-permute-done.32 = bf16[1024,384]{1,0:T(8,128)(2,1)S(1)} collective-permute-done((bf16[1024,384]{1,0:T(8,128)(2,1)S(1)}, bf16[1024,384]{1,0:T(8,128)(2,1)S(1)}, u32[]{:S(2)}, u32[]{:S(2)}) %collective-permute-start.32) | collective-permute-done | bytes 786464 | tf_op jit(solution)/shard_map/ppermute | solution.py:175
  362.2 15.8 %collective-permute-done.35 = bf16[1024,384]{1,0:T(8,128)(2,1)S(1)} collective-permute-done((bf16[1024,384]{1,0:T(8,128)(2,1)S(1)}, bf16[1024,384]{1,0:T(8,128)(2,1)S(1)}, u32[]{:S(2)}, u32[]{:S(2)}) %collective-permute-start.35) | collective-permute-done | bytes 786464 | tf_op jit(solution)/shard_map/ppermute | solution.py:175
  388.9 23.6 %collective-permute-done.6 = bf16[1024,384]{1,0:T(8,128)(2,1)S(1)} collective-permute-done((bf16[1024,384]{1,0:T(8,128)(2,1)S(1)}, bf16[1024,384]{1,0:T(8,128)(2,1)S(1)}, u32[]{:S(2)}, u32[]{:S(2)}) %collective-permute-start.6) | collective-permute-done | bytes 786464 | tf_op jit(solution)/shard_map/ppermute | solution.py:175
  414.1 15.4 %collective-permute-done.10 = bf16[1024,384]{1,0:T(8,128)(2,1)S(1)} collective-permute-done((bf16[1024,384]{1,0:T(8,128)(2,1)S(1)}, bf16[1024,384]{1,0:T(8,128)(2,1)S(1)}, u32[]{:S(2)}, u32[]{:S(2)}) %collective-permute-start.10) | collective-permute-done | bytes 786464 | tf_op jit(solution)/shard_map/ppermute | solution.py:175
  430.9 15.4 %collective-permute-done.16 = bf16[1024,384]{1,0:T(8,128)(2,1)S(1)} collective-permute-done((bf16[1024,384]{1,0:T(8,128)(2,1)S(1)}, bf16[1024,384]{1,0:T(8,128)(2,1)S(1)}, u32[]{:S(2)}, u32[]{:S(2)}) %collective-permute-start.16) | collective-permute-done | bytes 786464 | tf_op jit(solution)/shard_map/ppermute | solution.py:175
  448.0 15.1 %collective-permute-done.19 = bf16[1024,384]{1,0:T(8,128)(2,1)S(1)} collective-permute-done((bf16[1024,384]{1,0:T(8,128)(2,1)S(1)}, bf16[1024,384]{1,0:T(8,128)(2,1)S(1)}, u32[]{:S(2)}, u32[]{:S(2)}) %collective-permute-start.19) | collective-permute-done | bytes 786464 | tf_op jit(solution)/shard_map/ppermute | solution.py:175
  463.3 16.7 %collective-permute-done.25 = bf16[1024,384]{1,0:T(8,128)(2,1)S(1)} collective-permute-done((bf16[1024,384]{1,0:T(8,128)(2,1)S(1)}, bf16[1024,384]{1,0:T(8,128)(2,1)S(1)}, u32[]{:S(2)}, u32[]{:S(2)}) %collective-permute-start.25) | collective-permute-done | bytes 786464 | tf_op jit(solution)/shard_map/ppermute | solution.py:175
  480.2 16.7 %collective-permute-done.28 = bf16[1024,384]{1,0:T(8,128)(2,1)S(1)} collective-permute-done((bf16[1024,384]{1,0:T(8,128)(2,1)S(1)}, bf16[1024,384]{1,0:T(8,128)(2,1)S(1)}, u32[]{:S(2)}, u32[]{:S(2)}) %collective-permute-start.28) | collective-permute-done | bytes 786464 | tf_op jit(solution)/shard_map/ppermute | solution.py:175
  534.0 52.0 %all_to_all.10 = bf16[32,128,256]{2,1,0:T(8,128)(2,1)S(1)} all-to-all(bf16[32,128,256]{2,1,0:T(8,128)(2,1)S(1)} %bitcast.121), channel_id=1, replica_groups=mesh['z'=4,'x'=2,'y'=2,'c'=2] {'z','x','y','c'}, dimensions={0} | all-to-all | bytes 4194304 | tf_op jit(solution)/shard_map/all_to_all | solution.py:185
  (182 shorter events, 176.5 us)
Async XLA Ops:
  4.2 54.5 %all-to-all-start = ((bf16[4,128,2048]{1,2,0:T(8,128)(2,1)}), bf16[4,128,2048]{1,2,0:T(8,128)(2,1)S(1)}, u32[]{:S(2)}, u32[]{:S(2)}) async-start(bf16[4,128,2048]{1,2,0:T(8,128)(2,1)} %bitcast.120), calls=%async_computation | async-start | bytes 4194304 | tf_op jit(solution)/shard_map/all_to_all | solution.py:146
  66.1 111.5 %collective-permute-start.7 = (bf16[1024,768]{1,0:T(8,128)(2,1)}, bf16[1024,768]{1,0:T(8,128)(2,1)}, u32[]{:S(2)}, u32[]{:S(2)}) collective-permute-start(bf16[1024,768]{1,0:T(8,128)(2,1)} %bitcast_dynamic-update-slice_fusion.4), channel_id=1, source_target_pairs={{0,4},{4,0},{1,5},{5,1},{2,6},{6,2},{3,7},{7,3},{8,12},{12,8},{9,1... | collective-permute-start | bytes 4718600 | tf_op jit(solution)/shard_map/ppermute | solution.py:137
  66.6 111.5 %collective-permute-start.3 = (bf16[1024,768]{1,0:T(8,128)(2,1)}, bf16[1024,768]{1,0:T(8,128)(2,1)}, u32[]{:S(2)}, u32[]{:S(2)}) collective-permute-start(bf16[1024,768]{1,0:T(8,128)(2,1)} %get-tuple-element.45), channel_id=1, source_target_pairs={{0,4},{4,0},{1,5},{5,1},{2,6},{6,2},{3,7},{7,3},{8,12},{12,8},{9,1... | collective-permute-start | bytes 4718600 | tf_op jit(solution)/shard_map/ppermute | solution.py:137
  85.9 68.9 %collective-permute-start.11 = (bf16[128,2048]{1,0:T(8,128)(2,1)S(1)}, bf16[128,2048]{1,0:T(8,128)(2,1)}, u32[]{:S(2)}, u32[]{:S(2)}) collective-permute-start(bf16[128,2048]{1,0:T(8,128)(2,1)S(1)} %bitcast.137), channel_id=1, source_target_pairs={{0,4},{4,0},{1,5},{5,1},{2,6},{6,2},{3,7},{7,3},{8,12},{12,8},{9,1... | collective-permute-start | bytes 1572872 | tf_op jit(solution)/shard_map/ppermute | solution.py:103
  87.8 78.1 %collective-permute-start.20 = (bf16[128,2048]{1,0:T(8,128)(2,1)S(1)}, bf16[128,2048]{1,0:T(8,128)(2,1)S(1)}, u32[]{:S(2)}, u32[]{:S(2)}) collective-permute-start(bf16[128,2048]{1,0:T(8,128)(2,1)S(1)} %bitcast.132), channel_id=1, source_target_pairs={{0,4},{4,0},{1,5},{5,1},{2,6},{6,2},{3,7},{7,3},{8,12},{12,8},{9,1... | collective-permute-start | bytes 1572872 | tf_op jit(solution)/shard_map/ppermute | solution.py:103
  98.7 76.5 %collective-permute-start.29 = (bf16[128,2048]{1,0:T(8,128)(2,1)S(1)}, bf16[128,2048]{1,0:T(8,128)(2,1)S(1)}, u32[]{:S(2)}, u32[]{:S(2)}) collective-permute-start(bf16[128,2048]{1,0:T(8,128)(2,1)S(1)} %bitcast.127), channel_id=1, source_target_pairs={{0,4},{4,0},{1,5},{5,1},{2,6},{6,2},{3,7},{7,3},{8,12},{12,8},{9,1... | collective-permute-start | bytes 1572872 | tf_op jit(solution)/shard_map/ppermute | solution.py:103
  154.8 78.5 %collective-permute-start.2 = (bf16[512,2048]{1,0:T(8,128)(2,1)}, bf16[512,2048]{1,0:T(8,128)(2,1)}, u32[]{:S(2)}, u32[]{:S(2)}) collective-permute-start(bf16[512,2048]{1,0:T(8,128)(2,1)} %pad_maximum_fusion.4), channel_id=1, source_target_pairs={{0,1},{1,0},{2,3},{3,2},{4,5},{5,4},{6,7},{7,6},{8,9},{9,8},{10,11... | collective-permute-start | bytes 6291464 | tf_op jit(solution)/shard_map/ppermute | solution.py:103
  177.6 54.8 %collective-permute-start.30 = (bf16[256,2048]{1,0:T(8,128)(2,1)S(1)}, bf16[256,2048]{1,0:T(8,128)(2,1)S(1)}, u32[]{:S(2)}, u32[]{:S(2)}) collective-permute-start(bf16[256,2048]{1,0:T(8,128)(2,1)S(1)} %pad_maximum_fusion.12), channel_id=1, source_target_pairs={{0,2},{2,0},{1,3},{3,1},{4,6},{6,4},{5,7},{7,5},{8,10},{10,8},{9,1... | collective-permute-start | bytes 3145736 | tf_op jit(solution)/shard_map/ppermute | solution.py:103
  193.9 57.7 %collective-permute-start.13 = (bf16[512,2048]{1,0:T(8,128)(2,1)S(1)}, bf16[512,2048]{1,0:T(8,128)(2,1)S(1)}, u32[]{:S(2)}, u32[]{:S(2)}) collective-permute-start(bf16[512,2048]{1,0:T(8,128)(2,1)S(1)} %pad_maximum_fusion.5), channel_id=1, source_target_pairs={{0,1},{1,0},{2,3},{3,2},{4,5},{5,4},{6,7},{7,6},{8,9},{9,8},{10,11... | collective-permute-start | bytes 6291464 | tf_op jit(solution)/shard_map/ppermute | solution.py:103
  216.3 47.3 %collective-permute-start.22 = (bf16[512,2048]{1,0:T(8,128)(2,1)S(1)}, bf16[512,2048]{1,0:T(8,128)(2,1)S(1)}, u32[]{:S(2)}, u32[]{:S(2)}) collective-permute-start(bf16[512,2048]{1,0:T(8,128)(2,1)S(1)} %pad_maximum_fusion.6), channel_id=1, source_target_pairs={{0,1},{1,0},{2,3},{3,2},{4,5},{5,4},{6,7},{7,6},{8,9},{9,8},{10,11... | collective-permute-start | bytes 6291464 | tf_op jit(solution)/shard_map/ppermute | solution.py:103
  240.7 48.2 %collective-permute-start.4 = (bf16[1024,384]{1,0:T(8,128)(2,1)}, bf16[1024,384]{1,0:T(8,128)(2,1)}, u32[]{:S(2)}, u32[]{:S(2)}) collective-permute-start(bf16[1024,384]{1,0:T(8,128)(2,1)} %slice.157), channel_id=1, source_target_pairs={{0,8},{24,16},{1,9},{25,17},{2,10},{26,18},{3,11},{27,19},{4,12},{... | collective-permute-start | bytes 2359304 | tf_op jit(solution)/shard_map/ppermute | solution.py:175
  263.6 47.1 %collective-permute-start.17 = (bf16[1024,384]{1,0:T(8,128)(2,1)S(1)}, bf16[1024,384]{1,0:T(8,128)(2,1)}, u32[]{:S(2)}, u32[]{:S(2)}) collective-permute-start(bf16[1024,384]{1,0:T(8,128)(2,1)S(1)} %slice.154), channel_id=1, source_target_pairs={{0,8},{24,16},{1,9},{25,17},{2,10},{26,18},{3,11},{27,19},{4,12},{... | collective-permute-start | bytes 2359304 | tf_op jit(solution)/shard_map/ppermute | solution.py:175
  277.0 50.5 %collective-permute-start.23 = (bf16[1024,384]{1,0:T(8,128)(2,1)S(1)}, bf16[1024,384]{1,0:T(8,128)(2,1)S(1)}, u32[]{:S(2)}, u32[]{:S(2)}) collective-permute-start(bf16[1024,384]{1,0:T(8,128)(2,1)S(1)} %slice.153), channel_id=1, source_target_pairs={{0,8},{24,16},{1,9},{25,17},{2,10},{26,18},{3,11},{27,19},{4,12},{... | collective-permute-start | bytes 2359304 | tf_op jit(solution)/shard_map/ppermute | solution.py:175
  288.9 55.5 %collective-permute-start.26 = (bf16[1024,384]{1,0:T(8,128)(2,1)S(1)}, bf16[1024,384]{1,0:T(8,128)(2,1)S(1)}, u32[]{:S(2)}, u32[]{:S(2)}) collective-permute-start(bf16[1024,384]{1,0:T(8,128)(2,1)S(1)} %slice.152), channel_id=1, source_target_pairs={{0,8},{24,16},{1,9},{25,17},{2,10},{26,18},{3,11},{27,19},{4,12},{... | collective-permute-start | bytes 2359304 | tf_op jit(solution)/shard_map/ppermute | solution.py:175
  291.6 69.7 %collective-permute-start.32 = (bf16[1024,384]{1,0:T(8,128)(2,1)S(1)}, bf16[1024,384]{1,0:T(8,128)(2,1)S(1)}, u32[]{:S(2)}, u32[]{:S(2)}) collective-permute-start(bf16[1024,384]{1,0:T(8,128)(2,1)S(1)} %slice.151), channel_id=1, source_target_pairs={{0,8},{24,16},{1,9},{25,17},{2,10},{26,18},{3,11},{27,19},{4,12},{... | collective-permute-start | bytes 2359304 | tf_op jit(solution)/shard_map/ppermute | solution.py:175
  294.2 83.7 %collective-permute-start.35 = (bf16[1024,384]{1,0:T(8,128)(2,1)S(1)}, bf16[1024,384]{1,0:T(8,128)(2,1)S(1)}, u32[]{:S(2)}, u32[]{:S(2)}) collective-permute-start(bf16[1024,384]{1,0:T(8,128)(2,1)S(1)} %slice.150), channel_id=1, source_target_pairs={{0,8},{24,16},{1,9},{25,17},{2,10},{26,18},{3,11},{27,19},{4,12},{... | collective-permute-start | bytes 2359304 | tf_op jit(solution)/shard_map/ppermute | solution.py:175
  310.7 68.1 %collective-permute-start.5 = (bf16[1024,384]{1,0:T(8,128)(2,1)S(1)}, bf16[1024,384]{1,0:T(8,128)(2,1)S(1)}, u32[]{:S(2)}, u32[]{:S(2)}) collective-permute-start(bf16[1024,384]{1,0:T(8,128)(2,1)S(1)} %add_convert_fusion.23), channel_id=1, source_target_pairs={{8,16},{16,8},{9,17},{17,9},{10,18},{18,10},{11,19},{19,11},{12,20... | collective-permute-start | bytes 2359304 | tf_op jit(solution)/shard_map/ppermute | solution.py:175
  327.6 52.2 %collective-permute-start.9 = (bf16[1024,384]{1,0:T(8,128)(2,1)S(1)}, bf16[1024,384]{1,0:T(8,128)(2,1)S(1)}, u32[]{:S(2)}, u32[]{:S(2)}) collective-permute-start(bf16[1024,384]{1,0:T(8,128)(2,1)S(1)} %add_convert_fusion.20), channel_id=1, source_target_pairs={{8,16},{16,8},{9,17},{17,9},{10,18},{18,10},{11,19},{19,11},{12,20... | collective-permute-start | bytes 2359304 | tf_op jit(solution)/shard_map/ppermute | solution.py:175
  384.5 61.8 %collective-permute-start.16 = (bf16[1024,384]{1,0:T(8,128)(2,1)S(1)}, bf16[1024,384]{1,0:T(8,128)(2,1)S(1)}, u32[]{:S(2)}, u32[]{:S(2)}) collective-permute-start(bf16[1024,384]{1,0:T(8,128)(2,1)S(1)} %add_convert_fusion.16), channel_id=1, source_target_pairs={{16,24},{8,0},{17,25},{9,1},{18,26},{10,2},{19,27},{11,3},{20,28},... | collective-permute-start | bytes 2359304 | tf_op jit(solution)/shard_map/ppermute | solution.py:175
  386.0 77.2 %collective-permute-start.19 = (bf16[1024,384]{1,0:T(8,128)(2,1)S(1)}, bf16[1024,384]{1,0:T(8,128)(2,1)S(1)}, u32[]{:S(2)}, u32[]{:S(2)}) collective-permute-start(bf16[1024,384]{1,0:T(8,128)(2,1)S(1)} %add_convert_fusion.13), channel_id=1, source_target_pairs={{16,24},{8,0},{17,25},{9,1},{18,26},{10,2},{19,27},{11,3},{20,28},... | collective-permute-start | bytes 2359304 | tf_op jit(solution)/shard_map/ppermute | solution.py:175
  387.5 92.5 %collective-permute-start.25 = (bf16[1024,384]{1,0:T(8,128)(2,1)S(1)}, bf16[1024,384]{1,0:T(8,128)(2,1)S(1)}, u32[]{:S(2)}, u32[]{:S(2)}) collective-permute-start(bf16[1024,384]{1,0:T(8,128)(2,1)S(1)} %add_convert_fusion.10), channel_id=1, source_target_pairs={{16,24},{8,0},{17,25},{9,1},{18,26},{10,2},{19,27},{11,3},{20,28},... | collective-permute-start | bytes 2359304 | tf_op jit(solution)/shard_map/ppermute | solution.py:175
  412.6 84.3 %collective-permute-start.28 = (bf16[1024,384]{1,0:T(8,128)(2,1)S(1)}, bf16[1024,384]{1,0:T(8,128)(2,1)S(1)}, u32[]{:S(2)}, u32[]{:S(2)}) collective-permute-start(bf16[1024,384]{1,0:T(8,128)(2,1)S(1)} %add_convert_fusion.7), channel_id=1, source_target_pairs={{16,24},{8,0},{17,25},{9,1},{18,26},{10,2},{19,27},{11,3},{20,28},... | collective-permute-start | bytes 2359304 | tf_op jit(solution)/shard_map/ppermute | solution.py:175
  429.4 93.5 %collective-permute-start.34 = (bf16[1024,384]{1,0:T(8,128)(2,1)S(1)}, bf16[1024,384]{1,0:T(8,128)(2,1)S(1)}, u32[]{:S(2)}, u32[]{:S(2)}) collective-permute-start(bf16[1024,384]{1,0:T(8,128)(2,1)S(1)} %add_convert_fusion.4), channel_id=1, source_target_pairs={{16,24},{8,0},{17,25},{9,1},{18,26},{10,2},{19,27},{11,3},{20,28},... | collective-permute-start | bytes 2359304 | tf_op jit(solution)/shard_map/ppermute | solution.py:175
  446.3 82.3 %collective-permute-start.37 = (bf16[1024,384]{1,0:T(8,128)(2,1)S(1)}, bf16[1024,384]{1,0:T(8,128)(2,1)S(1)}, u32[]{:S(2)}, u32[]{:S(2)}) collective-permute-start(bf16[1024,384]{1,0:T(8,128)(2,1)S(1)} %add_convert_fusion.1), channel_id=1, source_target_pairs={{16,24},{8,0},{17,25},{9,1},{18,26},{10,2},{19,27},{11,3},{20,28},... | collective-permute-start | bytes 2359304 | tf_op jit(solution)/shard_map/ppermute | solution.py:175
  (27 other events, 463.2 us)
